TPU v7x, 128 devices: a whole 4x4x4 slice. The times are simulated.
128 devices in a mesh: grp: 16 (over z, x_lo, core), col: 8 (over x_hi, y).
Axes of the slice: x: 4 (x_hi: 2, x_lo: 2; x = x_hi * 2 + x_lo), y: 4, z: 4, core: 2. Of those that a mesh axis runs over, the one named last changes fastest.
Arguments:
- constraint_rows: float32 [4096, 16384], P('grp', 'col'), may hold values from -0.125 to 0.125
- shift: float32 [16384], P('col'), may hold values from 0.3 to 1
- group_rows: int32 [16], replicated, may hold values from 1 to 256, 2048 in all
- panel_index: int32 [1], replicated, may hold values from 0 to 31
Outputs:
- panel_factor: float32 [16384, 512], P(('col', 'grp'))
Inputs may be any that keep to these rules, and one draw needn't show every extreme that they name: `group_rows`: the values sum to 2048 and the largest equals 256.
All inputs are finite; a program needn't handle non-finite values.
Results may differ from a plain program's by a relative error of at most 0.000076.
Values sent between devices are 32-bit elements; how exact they have to be, the bound alone decides.
A program may use at most 64 MiB of HBM per device.

v0:
```python
import jax
import jax.numpy as jnp
from jax import lax
from jax.sharding import PartitionSpec as P

PANEL = 512


def picked(x, axis, root):
    return lax.dynamic_index_in_dim(lax.all_gather(x, axis), root, 0, keepdims=False)


def cut_along(x, dim, size):
    before, after = (x.shape[:dim], x.shape[dim + 1 :])
    return jnp.moveaxis(x.reshape(*before, size, -1, *after), dim, 0)


def sent_and_summed(x, axis, dim):
    pieces = cut_along(x, dim, lax.axis_size(axis))
    arrived = lax.all_to_all(pieces, axis, split_axis=0, concat_axis=0, tiled=True)
    return arrived.sum(axis=0)


def product(left, right):
    return lax.dot_general(
        left,
        right,
        (((0,), (0,)), ((), ())),
        precision=lax.Precision.HIGHEST,
        preferred_element_type=jnp.float32,
    )


def gram_rows(left, panel_cols):
    return product(left, panel_cols)


def add_shift(values, shift_part, first_row, start):
    row_ids = first_row + jnp.arange(values.shape[0], dtype=jnp.int32)
    col_ids = jnp.arange(values.shape[1], dtype=jnp.int32)
    on_diag = row_ids[:, None] == start + col_ids[None, :]
    return values + jnp.where(on_diag, shift_part[:, None], jnp.zeros_like(values))


def on_device(constraint_rows, shift, group_rows, panel_index):
    width = constraint_rows.shape[1]
    groups = lax.axis_size("grp")
    col_idx = lax.axis_index("col")
    grp_idx = lax.axis_index("grp")
    share = width // groups
    start = panel_index[0] * PANEL
    owner = start // width
    local = start - owner * width
    live_count = lax.dynamic_index_in_dim(group_rows, grp_idx, keepdims=False)
    row_ids = jnp.arange(constraint_rows.shape[0], dtype=jnp.int32)
    masked = jnp.where(
        (row_ids < live_count)[:, None], constraint_rows, jnp.zeros_like(constraint_rows)
    )
    own_cols = lax.dynamic_slice_in_dim(masked, local, PANEL, 1)
    panel_cols = picked(own_cols, "col", owner)
    mine = sent_and_summed(gram_rows(masked, panel_cols), "grp", 0)
    shift_part = lax.dynamic_slice_in_dim(shift, grp_idx * share, share, 0)
    mine = add_shift(mine, shift_part, col_idx * width + grp_idx * share, start)
    from_owner = picked(mine, "col", owner)
    owner_shard = lax.all_gather(from_owner, "grp", axis=0, tiled=True)
    block = lax.dynamic_slice_in_dim(owner_shard, local, PANEL, 0)
    factor = jnp.linalg.cholesky(block)
    return lax.linalg.triangular_solve(factor, mine, left_side=False, lower=True, transpose_a=True)


def solution(mesh):
    placed = (P("grp", "col"), P("col"), P(), P())
    return jax.shard_map(
        on_device, mesh=mesh, in_specs=placed, out_specs=P(("col", "grp"), None), check_vma=False
    )
```

profile of v0, /device:TPU:1, one launch (start us, length us, event | category | flops | bytes accessed | tf_op | source)
XLA Modules:
  0.0 386.7 jit_solution(9339683539107075784)
XLA Ops:
  7.2 1.2 dynamic_slice.21
  8.5 0.6 iota_compare_fusion.3
  9.1 1.9 broadcast_select_fusion
  11.1 0.9 constant_dynamic-slice_fusion.3
  12.0 1.5 fusion.41
  13.5 1.9 copy.12
  15.5 70.8 %all-gather.8.cloned.1.call-done = f32[2048,512]{1,0:T(8,128)} async-done(((f32[256,512]{1,0:T(8,128)}), f32[2048,512]{1,0:T(8,128)}) %all-gather.8.cloned.1.call-update) | async-done | bytes 4194320 | tf_op jit(solution)/shard_map/all_gather | solution.py:10
  86.2 6.0 %fusion.1 = f32[16,128,512]{2,1,0:T(8,128)} fusion(f32[16,128,256]{2,1,0:T(8,128)S(1)} %bitcast.65, f32[8,256,512]{2,1,0:T(8,128)} %bitcast.66, s32[]{:T(128)S(6)} %select_n.47), kind=kOutput, calls=%fused_computation.15 | convolution fusion | flops 3221225472 | bytes 6815748 | tf_op jit(solution)/shard_map/dot_general | solution.py:25
  92.3 5.5 %all-to-all-start = ((f32[16,128,512]{2,1,0:T(8,128)}), f32[16,128,512]{2,1,0:T(8,128)}, u32[]{:S(2)}, u32[]{:S(2)}) async-start(f32[16,128,512]{2,1,0:T(8,128)} %fusion.1), calls=%async_computation | async-start | bytes 8388608 | tf_op jit(solution)/shard_map/all_to_all | solution.py:20
  97.8 0.8 dynamic_slice.24
  98.6 48.9 %all-to-all-done = f32[16,128,512]{2,1,0:T(8,128)} async-done(((f32[16,128,512]{2,1,0:T(8,128)}), f32[16,128,512]{2,1,0:T(8,128)}, u32[]{:S(2)}, u32[]{:S(2)}) %all-to-all-start) | async-done | bytes 4194336 | tf_op jit(solution)/shard_map/all_to_all | solution.py:20
  147.5 2.6 reduce_sum.11
  150.1 0.8 bitcast_add_fusion.1
  151.2 50.8 %all-gather.6.cloned.1.call-done = f32[8,128,512]{2,1,0:T(8,128)} async-done(((f32[1,128,512]{2,1,0:T(8,128)}), f32[8,128,512]{2,1,0:T(8,128)}) %all-gather.6.cloned.1.call-update) | async-done | bytes 2097168 | tf_op jit(solution)/shard_map/all_gather | solution.py:10
  201.9 1.7 constant_dynamic-slice_fusion.2
  203.7 36.2 %all-gather.10.cloned.1.call-done = f32[1,2048,512]{2,1,0:T(8,128)} async-done(((f32[1,128,512]{2,1,0:T(8,128)}), f32[1,2048,512]{2,1,0:T(8,128)}) %all-gather.10.cloned.1.call-update) | async-done | bytes 4194320 | tf_op jit(solution)/shard_map/all_gather | solution.py:65
  239.9 1.3 constant_dynamic-slice_fusion.1
  241.2 0.3 copy.9
  241.5 1.5 fusion
  243.0 11.7 %cholesky.104 = f32[128,128]{1,0:T(8,128)S(1)} custom-call(f32[128,128]{1,0:T(8,128)S(1)} %cholesky.266), custom_call_target="Cholesky" | custom-call | tf_op jit(solution)/shard_map/jit(cholesky)/cholesky | solution.py:67
  254.9 9.8 %custom-call.30 = f32[1,128,128]{1,2,0:T(8,128)S(1)} custom-call(f32[1,128,128]{2,1,0:T(8,128)S(1)} %get-tuple-element.32), custom_call_target="InvertDiagBlocksLowerTriangular" | custom-call | tf_op jit(solution)/shard_map/jit(cholesky)/cholesky | solution.py:67
  264.7 0.3 constant_dynamic-update-slice_fusion
  265.0 0.3 convolution_subtract_fusion
  265.4 11.7 %cholesky.217 = f32[128,128]{1,0:T(8,128)S(1)} custom-call(f32[128,128]{1,0:T(8,128)S(1)} %cholesky.270), custom_call_target="Cholesky" | custom-call | tf_op jit(solution)/shard_map/jit(cholesky)/cholesky | solution.py:67
  277.1 10.0 %custom-call.31 = f32[1,128,128]{1,2,0:T(8,128)S(1)} custom-call(f32[1,128,128]{2,1,0:T(8,128)S(1)} %get-tuple-element.29), custom_call_target="InvertDiagBlocksLowerTriangular" | custom-call | tf_op jit(solution)/shard_map/jit(cholesky)/cholesky | solution.py:67
  287.4 0.4 convolution_subtract_fusion.1
  287.8 11.7 %cholesky.238 = f32[128,128]{1,0:T(8,128)S(1)} custom-call(f32[128,128]{1,0:T(8,128)S(1)} %cholesky.275), custom_call_target="Cholesky" | custom-call | tf_op jit(solution)/shard_map/jit(cholesky)/cholesky | solution.py:67
  299.5 0.6 compare_reduce_fusion.1
  300.2 9.8 %custom-call.32 = f32[1,128,128]{1,2,0:T(8,128)S(1)} custom-call(f32[1,128,128]{2,1,0:T(8,128)S(1)} %get-tuple-element.26), custom_call_target="InvertDiagBlocksLowerTriangular" | custom-call | tf_op jit(solution)/shard_map/jit(cholesky)/cholesky | solution.py:67
  310.2 0.4 convolution_subtract_fusion.5
  310.6 11.7 %cholesky.255 = f32[128,128]{1,0:T(8,128)S(1)} custom-call(f32[128,128]{1,0:T(8,128)S(1)} %convolution_subtract_fusion.5), custom_call_target="Cholesky" | custom-call | tf_op jit(solution)/shard_map/jit(cholesky)/cholesky | solution.py:67
  322.3 0.9 compare_reduce_fusion
  323.3 0.7 compare_reduce_fusion.2
  326.6 10.1 %while.1 = (s32[]{:T(128)}, f32[512,512]{1,0:T(8,128)S(1)}, s32[4,2]{0,1:T(2,128)S(1)}, f32[4,128,128]{2,1,0:T(8,128)}, s32[]{:T(128)}) while((s32[]{:T(128)}, f32[512,512]{1,0:T(8,128)S(1)}, s32[4,2]{0,1:T(2,128)S(1)}, f32[4,128,128]{2,1,0:T(8,128)}, s32[]{:T(128)}) %tuple.27), condition=%wide.while_cond, body=%wide.while_body.sunk | while | flops 2 | bytes 132705 | solution.py:68
  326.7 0.5 fusion.43
  327.2 1.9 bitcast_dynamic-update-slice_fusion.2
  329.3 0.5 fusion.43
  329.8 1.9 bitcast_dynamic-update-slice_fusion.2
  331.8 0.5 fusion.43
  332.3 1.9 bitcast_dynamic-update-slice_fusion.2
  334.3 0.5 fusion.43
  334.8 1.9 bitcast_dynamic-update-slice_fusion.2
  336.8 40.1 %custom-call.33 = f32[4,128,128]{1,2,0:T(8,128)S(1)} custom-call(f32[4,128,128]{2,1,0:T(8,128)} %get-tuple-element.12), custom_call_target="InvertDiagBlocksLowerTriangular" | custom-call | tf_op jit(solution)/shard_map/triangular_solve | solution.py:68
  376.9 0.3 fusion.24
  377.8 0.4 convolution_subtract_fusion.2
  378.2 0.3 fusion.21
  378.5 0.5 convolution_subtract_fusion.4
  379.3 0.8 copy.11
  (33 shorter events, 2.5 us)
Async XLA Ops:
  6.5 79.7 %all-gather.8.cloned.1.call-start = ((), (), s32[]{:S(2)}) async-start(), calls=%async_computation.2 | async-start | bytes 4718592 | tf_op jit(solution)/shard_map/all_gather | solution.py:10
  9.1 2.9 copy-start
  92.3 55.2 %all-to-all-start = ((f32[16,128,512]{2,1,0:T(8,128)}), f32[16,128,512]{2,1,0:T(8,128)}, u32[]{:S(2)}, u32[]{:S(2)}) async-start(f32[16,128,512]{2,1,0:T(8,128)} %fusion.1), calls=%async_computation | async-start | bytes 8388608 | tf_op jit(solution)/shard_map/all_to_all | solution.py:20
  97.8 104.1 %all-gather.6.cloned.1.call-start = ((), (), s32[]{:S(2)}) async-start(), calls=%async_computation.1 | async-start | bytes 2359296 | tf_op jit(solution)/shard_map/all_gather | solution.py:10
  150.9 89.0 %all-gather.10.cloned.1.call-start = ((), (), s32[]{:S(2)}) async-start(), calls=%async_computation.3 | async-start | bytes 4456448 | tf_op jit(solution)/shard_map/all_gather | solution.py:65
Sparse Core Ops, SparseCore 0:
  12.1 74.0 all-gather.7
  151.1 50.8 all-gather.5
  203.7 36.1 all-gather.9
where the time goes:
time: 387 us
  waiting for transfers between devices  207 us (53%)
  other arithmetic  128 us (33%)
  local copies, waits for them, and re-layouts  19.2 us (5%)
  between operations  16.6 us (4%)
  matrix products  10.2 us (3%)
  starting transfers between devices  5.78 us (1%)
    all_gather x2, waiting for transfers between devices, picked(): lax.all_gather(x, axis)  122 us
    another operation x14, other arithmetic, on_device(): factor = jnp.linalg.cholesky(block)  78.8 us
    all_to_all x1, waiting for transfers between devices, sent_and_summed(): lax.all_to_all(pieces, axis, split_axis=0, concat_axis=0, tiled=True)  48.9 us
    another operation x4, other arithmetic, on_device(): lax.linalg.triangular_solve(factor, mine, left_side=False, lower=True, tr...  40.3 us
    all_gather x1, waiting for transfers between devices, on_device(): owner_shard = lax.all_gather(from_owner, 'grp', axis=0, tiled=True)  36.2 us
    another operation x12, local copies, waits for them, and re-layouts  10.1 us
  transfers between devices with their start and end apart: 4, of which 4 were waited for; matrix products, arithmetic and copies ran while one was open for 1% of the time, Pallas kernels for 0%

commit v1 on v0

--- a/solution.py
+++ b/solution.py
@@ -1,9 +1,101 @@
-import jax
-import jax.numpy as jnp
+import jax, jax.numpy as jnp
 from jax import lax
+from jax.experimental import pallas as pl
+from jax.experimental.pallas import tpu as pltpu
+
 from jax.sharding import PartitionSpec as P
 
 PANEL = 512
+
+
+B = 128
+HI = lax.Precision.HIGHEST
+
+
+def inv_chol(rows):
+    lane = lax.broadcasted_iota(jnp.int32, (8, B), 1)
+    rows = list(rows)
+    for s in range(16):
+        k0 = 8 * s
+        inside = (lane >= k0) & (lane < k0 + 8)
+        tile = rows[s]
+        spread = lambda t, l: jnp.broadcast_to(t[:, k0 + l : k0 + l + 1], (8, B))
+        cols = [spread(tile, l) for l in range(8)]
+        c = {(m, l): jnp.broadcast_to(cols[l][m : m + 1, :], (8, B)) for l in range(8) for m in range(l, 8)}
+        r = [
+            jnp.where(inside, jnp.where(lane == k0 + m, 1.0, 0.0), jnp.broadcast_to(tile[m : m + 1, :], (8, B)))
+            for m in range(8)
+        ]
+        rs, low = {}, {}
+        for j in range(8):
+            rs[j] = lax.rsqrt(c[j, j])
+            r[j] = r[j] * rs[j]
+            for m in range(j + 1, 8):
+                low[m, j] = c[m, j] * rs[j]
+            for m in range(j + 1, 8):
+                for n in range(j + 1, m + 1):
+                    c[m, n] = c[m, n] - low[m, j] * low[n, j]
+                r[m] = r[m] - low[m, j] * r[j]
+        sub = lax.broadcasted_iota(jnp.int32, (8, B), 0)
+        done = r[0]
+        for j in range(1, 8):
+            done = jnp.where(sub == j, r[j], done)
+        rows[s] = jnp.where(lane < k0 + 8, done, 0.0)
+        if s < 15:
+            g = list(r)
+            for j in reversed(range(8)):
+                for m in range(j + 1, 8):
+                    g[j] = g[j] - low[m, j] * g[m]
+                g[j] = g[j] * rs[j]
+            for i in range(s + 1, 16):
+                f = [spread(rows[i], l) for l in range(8)]
+                t = jnp.where(inside, 0.0, rows[i])
+                p0 = f[0] * g[0] + f[1] * g[1]
+                p1 = f[2] * g[2] + f[3] * g[3]
+                p2 = f[4] * g[4] + f[5] * g[5]
+                p3 = f[6] * g[6] + f[7] * g[7]
+                rows[i] = t - ((p0 + p1) + (p2 + p3))
+    return rows
+
+
+def dot(a, b, dims=((1,), (0,))):
+    return lax.dot_general(a, b, (dims, ((), ())), precision=HI, preferred_element_type=jnp.float32)
+
+
+def factor_and_solve(m_ref, blocks):
+    n = blocks * B
+    width = m_ref.shape[1]
+    for k in range(blocks):
+        at = k * B
+        w = jnp.concatenate(inv_chol([m_ref[at + 8 * i : at + 8 * i + 8, at : at + B] for i in range(16)]), axis=0)
+        u = dot(w, m_ref[at : at + B, at + B :])
+        if k == blocks - 1:
+            return u
+        m_ref[at : at + B, at + B :] = u
+        for r in range(k + 1, blocks):
+            left = u[:, (r - k - 1) * B : (r - k) * B]
+            m_ref[r * B : (r + 1) * B, r * B :] -= dot(left, u[:, (r - k - 1) * B :], ((0,), (0,)))
+
+
+def solve_kernel(d_ref, t_ref, x_ref, m_ref):
+    n = d_ref.shape[0]
+    m_ref[:, :n] = d_ref[...]
+    m_ref[:, n:] = t_ref[...]
+    blocks = n // B
+    last = factor_and_solve(m_ref, blocks)
+    for k in range(blocks):
+        block = last if k == blocks - 1 else m_ref[k * B : (k + 1) * B, n:]
+        x_ref[:, k * B : (k + 1) * B] = block.T
+
+
+def solve(d, t):
+    n, w = d.shape[0], t.shape[1]
+    return pl.pallas_call(
+        solve_kernel,
+        out_shape=jax.ShapeDtypeStruct((w, n), jnp.float32),
+        scratch_shapes=[pltpu.VMEM((n, n + w), jnp.float32)],
+        compiler_params=pltpu.CompilerParams(vmem_limit_bytes=32 << 20),
+    )(d, t)
 
 
 def picked(x, axis, root):
@@ -64,8 +156,7 @@
     from_owner = picked(mine, "col", owner)
     owner_shard = lax.all_gather(from_owner, "grp", axis=0, tiled=True)
     block = lax.dynamic_slice_in_dim(owner_shard, local, PANEL, 0)
-    factor = jnp.linalg.cholesky(block)
-    return lax.linalg.triangular_solve(factor, mine, left_side=False, lower=True, transpose_a=True)
+    return solve(block, mine.T)
 
 
 def solution(mesh):

time: 387 us -> 275 us (0.71)
  other arithmetic: 128 us -> 7.71 us
  Pallas kernels: 0 us -> 26.8 us
  local copies, waits for them, and re-layouts: 19.2 us -> 7.89 us
  matrix products: 10.2 us -> 6.01 us
    another operation x18 -> x0, other arithmetic: 119 us -> none  [the longest x14 78.8 us: on_device(): factor = jnp.linalg.cholesky(block)]
    pallas_call x0 -> x1, Pallas kernels: none -> 26.8 us  [solve(): pl.pallas_call(solve_kernel, out_shape=jax.ShapeDtypeStruct((w, n), jnp.f...]
    another operation x18 -> x0, local copies, waits for them, and re-layouts: 11.1 us -> none
    another operation x13 -> x0, matrix products: 4.18 us -> none  [the longest x7 2.31 us: on_device(): lax.linalg.triangular_solve(factor, mine, left_side=False, lower=True, tr...]
  transfers between devices with their start and end apart: 4 -> 4, of which waited for: 4 -> 4; matrix products, arithmetic and copies ran while one was open for 1% -> 2% of each run, Pallas kernels for 0% -> 0%
where the time goes in v1:
time: 275 us
  waiting for transfers between devices  206 us (75%)
  Pallas kernels  26.8 us (10%)
  between operations  13.9 us (5%)
  local copies, waits for them, and re-layouts  7.89 us (3%)
  other arithmetic  7.71 us (3%)
  matrix products  6.01 us (2%)
  starting transfers between devices  5.79 us (2%)
    all_gather x2, waiting for transfers between devices, picked(): lax.all_gather(x, axis)  122 us
    all_to_all x1, waiting for transfers between devices, sent_and_summed(): lax.all_to_all(pieces, axis, split_axis=0, concat_axis=0, tiled=True)  48.9 us
    all_gather x1, waiting for transfers between devices, on_device(): owner_shard = lax.all_gather(from_owner, 'grp', axis=0, tiled=True)  36 us
    pallas_call x1, Pallas kernels, solve(): pl.pallas_call(solve_kernel, out_shape=jax.ShapeDtypeStruct((w, n), jnp.f...  26.8 us
    dot_general x1, matrix products, product(): lax.dot_general(left, right, (((0,), (0,)), ((), ())), precision=lax.Prec...  6.01 us
    all_to_all x1, starting transfers between devices, sent_and_summed(): lax.all_to_all(pieces, axis, split_axis=0, concat_axis=0, tiled=True)  5.53 us
  transfers between devices with their start and end apart: 4, of which 4 were waited for; matrix products, arithmetic and copies ran while one was open for 2% of the time, Pallas kernels for 0%

profile of v1, /device:TPU:1, one launch (start us, length us, event | category | flops | bytes accessed | tf_op | source)
XLA Modules:
  0.0 274.6 jit_solution(5046252351709479774)
XLA Ops:
  6.5 0.0 all-gather.8.cloned.1.call-start
  7.2 1.2 dynamic_slice.21
  8.5 0.6 iota_compare_fusion
  9.1 0.0 copy-start
  9.1 1.9 broadcast_select_fusion
  11.1 0.9 constant_dynamic-slice_fusion.1
  12.0 0.0 all-gather.8.cloned.1.call-update
  12.0 0.0 copy-done
  12.0 1.5 fusion.5
  13.5 1.9 copy.10
  15.5 70.8 %all-gather.8.cloned.1.call-done = f32[2048,512]{1,0:T(8,128)} async-done(((f32[256,512]{1,0:T(8,128)}), f32[2048,512]{1,0:T(8,128)}) %all-gather.8.cloned.1.call-update) | async-done | bytes 4194320 | tf_op jit(solution)/shard_map/all_gather | solution.py:102
  86.2 6.0 %fusion = f32[16,128,512]{2,1,0:T(8,128)} fusion(f32[16,128,256]{2,1,0:T(8,128)S(1)} %bitcast.17, f32[8,256,512]{2,1,0:T(8,128)} %bitcast.18, s32[]{:T(128)S(6)} %select_n.44), kind=kOutput, calls=%fused_computation.2 | convolution fusion | flops 3221225472 | bytes 6815748 | tf_op jit(solution)/shard_map/dot_general | solution.py:117
  92.3 5.5 %all-to-all-start = ((f32[16,128,512]{2,1,0:T(8,128)}), f32[16,128,512]{2,1,0:T(8,128)}, u32[]{:S(2)}, u32[]{:S(2)}) async-start(f32[16,128,512]{2,1,0:T(8,128)} %fusion), calls=%async_computation | async-start | bytes 8388608 | tf_op jit(solution)/shard_map/all_to_all | solution.py:112
  97.8 0.0 all-gather.6.cloned.1.call-start
  97.8 0.8 dynamic_slice.24
  98.6 48.9 %all-to-all-done = f32[16,128,512]{2,1,0:T(8,128)} async-done(((f32[16,128,512]{2,1,0:T(8,128)}), f32[16,128,512]{2,1,0:T(8,128)}, u32[]{:S(2)}, u32[]{:S(2)}) %all-to-all-start) | async-done | bytes 4194336 | tf_op jit(solution)/shard_map/all_to_all | solution.py:112
  147.5 2.6 reduce_sum.13
  150.1 0.8 bitcast_add_fusion.1
  150.9 0.0 all-gather.6.cloned.1.call-update
  150.9 0.2 all-gather.10.cloned.1.call-start
  151.2 50.7 %all-gather.6.cloned.1.call-done = f32[8,128,512]{2,1,0:T(8,128)} async-done(((f32[1,128,512]{2,1,0:T(8,128)}), f32[8,128,512]{2,1,0:T(8,128)}) %all-gather.6.cloned.1.call-update) | async-done | bytes 2097168 | tf_op jit(solution)/shard_map/all_gather | solution.py:102
  201.9 1.7 constant_dynamic-slice_fusion
  203.6 0.0 all-gather.10.cloned.1.call-update
  203.6 0.1 copy.9
  203.7 0.1 bitcast_add_fusion.t_ref
  203.9 36.0 %all-gather.10.cloned.1.call-done = f32[1,2048,512]{2,1,0:T(8,128)} async-done(((f32[1,128,512]{2,1,0:T(8,128)}), f32[1,2048,512]{2,1,0:T(8,128)}) %all-gather.10.cloned.1.call-update) | async-done | bytes 4194320 | tf_op jit(solution)/shard_map/all_gather | solution.py:157
  239.9 1.3 dynamic-slice_bitcast_fusion.d_ref
  241.2 26.8 %shard_map.46 = f32[128,512]{1,0:T(8,128)} custom-call(f32[512,512]{1,0:T(8,128)S(1)} %dynamic-slice_bitcast_fusion.d_ref, f32[512,128]{1,0:T(8,128)S(1)} %bitcast_add_fusion.t_ref), custom_call_target="tpu_custom_call" | custom-call | tf_op jit(solution)/shard_map/pallas_call | solution.py:93
  (2 shorter events, 0.0 us)
Async XLA Ops:
  6.5 79.7 %all-gather.8.cloned.1.call-start = ((), (), s32[]{:S(2)}) async-start(), calls=%async_computation.2 | async-start | bytes 4718592 | tf_op jit(solution)/shard_map/all_gather | solution.py:102
  9.1 2.9 %copy-start = (f32[256,2048]{1,0:T(8,128)S(1)}, f32[256,2048]{1,0:T(8,128)}, u32[]{:S(2)}) copy-start(f32[256,2048]{1,0:T(8,128)} %param.4) | copy-start | bytes 6291460
  92.3 55.2 %all-to-all-start = ((f32[16,128,512]{2,1,0:T(8,128)}), f32[16,128,512]{2,1,0:T(8,128)}, u32[]{:S(2)}, u32[]{:S(2)}) async-start(f32[16,128,512]{2,1,0:T(8,128)} %fusion), calls=%async_computation | async-start | bytes 8388608 | tf_op jit(solution)/shard_map/all_to_all | solution.py:112
  97.8 104.1 %all-gather.6.cloned.1.call-start = ((), (), s32[]{:S(2)}) async-start(), calls=%async_computation.1 | async-start | bytes 2359296 | tf_op jit(solution)/shard_map/all_gather | solution.py:102
  150.9 89.0 %all-gather.10.cloned.1.call-start = ((), (), s32[]{:S(2)}) async-start(), calls=%async_computation.3 | async-start | bytes 4456448 | tf_op jit(solution)/shard_map/all_gather | solution.py:157
Sparse Core Ops, SparseCore 0:
  12.1 74.0 all-gather.7
  151.1 50.8 all-gather.5
  203.7 36.1 all-gather.9

commit v2 on v1

--- a/solution.py
+++ b/solution.py
@@ -2,11 +2,7 @@
 from jax import lax
 from jax.experimental import pallas as pl
 from jax.experimental.pallas import tpu as pltpu
-
 from jax.sharding import PartitionSpec as P
-
-PANEL = 512
-
 
 B = 128
 HI = lax.Precision.HIGHEST
@@ -78,10 +74,11 @@
 
 
 def solve_kernel(d_ref, t_ref, x_ref, m_ref):
-    n = d_ref.shape[0]
-    m_ref[:, :n] = d_ref[...]
+    n, w = t_ref.shape
+    blocks = n // B
+    for k in range(blocks):
+        m_ref[k * B : (k + 1) * B, k * B : n] = d_ref[:, OFFSETS[k] : OFFSETS[k] + n - k * B]
     m_ref[:, n:] = t_ref[...]
-    blocks = n // B
     last = factor_and_solve(m_ref, blocks)
     for k in range(blocks):
         block = last if k == blocks - 1 else m_ref[k * B : (k + 1) * B, n:]
@@ -89,7 +86,7 @@
 
 
 def solve(d, t):
-    n, w = d.shape[0], t.shape[1]
+    n, w = t.shape
     return pl.pallas_call(
         solve_kernel,
         out_shape=jax.ShapeDtypeStruct((w, n), jnp.float32),
@@ -98,65 +95,220 @@
     )(d, t)
 
 
-def picked(x, axis, root):
-    return lax.dynamic_index_in_dim(lax.all_gather(x, axis), root, 0, keepdims=False)
-
-
-def cut_along(x, dim, size):
-    before, after = (x.shape[:dim], x.shape[dim + 1 :])
-    return jnp.moveaxis(x.reshape(*before, size, -1, *after), dim, 0)
-
-
-def sent_and_summed(x, axis, dim):
-    pieces = cut_along(x, dim, lax.axis_size(axis))
-    arrived = lax.all_to_all(pieces, axis, split_axis=0, concat_axis=0, tiled=True)
-    return arrived.sum(axis=0)
-
-
-def product(left, right):
-    return lax.dot_general(
-        left,
-        right,
-        (((0,), (0,)), ((), ())),
-        precision=lax.Precision.HIGHEST,
-        preferred_element_type=jnp.float32,
-    )
-
-
-def gram_rows(left, panel_cols):
-    return product(left, panel_cols)
-
-
-def add_shift(values, shift_part, first_row, start):
-    row_ids = first_row + jnp.arange(values.shape[0], dtype=jnp.int32)
-    col_ids = jnp.arange(values.shape[1], dtype=jnp.int32)
-    on_diag = row_ids[:, None] == start + col_ids[None, :]
-    return values + jnp.where(on_diag, shift_part[:, None], jnp.zeros_like(values))
+GROUP_ROWS = 256
+WIDTH = 2048
+PANEL = 512
+CHIPS = 8
+COLS = 8
+PIECE = GROUP_ROWS // COLS
+SHARE = 128
+OFFSETS = [0, 512, 896, 1152]
+PACKED = 1280
+MESH = pl.DeviceIdType.MESH
+
+
+def where_am_i():
+    grp, col = lax.axis_index("grp"), lax.axis_index("col")
+    return grp, col, lax.rem(grp, 2), grp // 2
+
+
+def chip_peer(chip, step):
+    z = lax.rem(chip // 2 + step // 2, 4)
+    x = lax.rem(lax.rem(chip, 2) + step % 2, 2)
+    return z * 2 + x
+
+
+def col_peer(col, step):
+    x = lax.rem(col // 4 + step // 4, 2)
+    y = lax.rem(lax.rem(col, 4) + step % 4, 4)
+    return x * 4 + y
+
+
+def choose(index, arrays):
+    chosen = arrays[0]
+    for i in range(1, len(arrays)):
+        chosen = jnp.where(index == i, arrays[i], chosen)
+    return chosen
+
+
+CHIP_STEPS = [5, 4, 3, 7, 2, 6, 1]
+COL_STEPS = [6, 2, 5, 7, 1, 3, 4]
+
+
+def gather_kernel(
+    groups_ref, panel_ref, b_ref, shift_ref, d_ref, t_ref,
+    own, scat, panel, panel_t, pack, pack_in, strips, strip_cols, part, other, other_in, landed,
+    scat_s, scat_r, ag_s, ag_r, dcore_s, dcore_r, drs_s, drs_r, dcol_s, dcol_r, dag_s, dag_r, dsib_s, dsib_r,
+    core_s, core_r, rs_s, rs_r,
+):
+    grp, col, core, chip = where_am_i()
+    sibling = {"grp": chip * 2 + (1 - core)}
+
+    def at_chip(step):
+        return {"grp": chip_peer(chip, step) * 2 + core}
+
+    def at_col(step):
+        return {"col": col_peer(col, step)}
+
+    barrier = pltpu.get_barrier_semaphore()
+    pl.semaphore_signal(barrier, 1, device_id=sibling, device_id_type=MESH)
+    for step in range(1, CHIPS):
+        pl.semaphore_signal(barrier, 1, device_id=at_chip(step), device_id_type=MESH)
+    for step in range(1, COLS):
+        pl.semaphore_signal(barrier, 1, device_id=at_col(step), device_id_type=MESH)
+
+    sends = []
+
+    def send(src, dst, s, r, to):
+        copy = pltpu.make_async_remote_copy(
+            src_ref=src, dst_ref=dst, send_sem=s, recv_sem=r, device_id=to, device_id_type=MESH
+        )
+        copy.start()
+        sends.append(copy)
+        return copy
+
+    owner = panel_ref[0] // 4
+    local = lax.rem(panel_ref[0], 4)
+    live = groups_ref[grp]
+    row = lax.broadcasted_iota(jnp.int32, (GROUP_ROWS, PANEL), 0)
+    own[...] = jnp.where(row < live, choose(local, [b_ref[:, k * PANEL : (k + 1) * PANEL] for k in range(4)]), 0.0)
+
+    pl.semaphore_wait(barrier, 15)
+
+    mine_rows = pl.ds(pl.multiple_of(col * PIECE, PIECE), PIECE)
+    scatters = []
+    for i, step in enumerate(COL_STEPS):
+        peer = col_peer(col, step)
+        scatters.append(send(
+            own.at[pl.ds(pl.multiple_of(peer * PIECE, PIECE), PIECE)], scat.at[col],
+            scat_s.at[i], scat_r.at[i], at_col(step)))
+    scat[col] = own[mine_rows, :]
+
+    for k in range(4):
+        pack[:, OFFSETS[k] : OFFSETS[k] + PANEL - k * B] = dot(
+            own[:, k * B : (k + 1) * B], own[:, k * B :], ((0,), (0,)))
+    half = pl.ds(pl.multiple_of(core * 64, 64), 64)
+    half_other = pl.ds(pl.multiple_of((1 - core) * 64, 64), 64)
+    swap = send(pack.at[half_other], pack_in, dcore_s, dcore_r, sibling)
+    swap.wait_recv()
+    pack[half, :] += pack_in[...]
+    reduces = []
+    for i, step in enumerate(CHIP_STEPS):
+        peer = chip_peer(chip, step)
+        reduces.append(send(
+            pack.at[pl.ds(pl.multiple_of(core * 64 + peer * 8, 8), 8)], strips.at[i],
+            drs_s.at[i], drs_r.at[i], at_chip(step)))
+
+    for copy in scatters:
+        copy.wait_recv()
+    panel[mine_rows, :] = choose(owner, [scat[c] for c in range(COLS)])
+    gathers = []
+    for i, step in enumerate(COL_STEPS):
+        gathers.append(send(panel.at[mine_rows], panel.at[mine_rows], ag_s.at[i], ag_r.at[i], at_col(step)))
+
+    strip_at = pl.multiple_of(core * 64 + chip * 8, 8)
+    strip_rows = pl.ds(strip_at, 8)
+    total = pack[strip_rows, :]
+    for i, copy in enumerate(reduces):
+        copy.wait_recv()
+        total += strips[i]
+    lane = lax.broadcasted_iota(jnp.int32, (8, B), 1)
+    sub = lax.broadcasted_iota(jnp.int32, (8, B), 0)
+    for k in range(4):
+        terms = choose(local, [shift_ref[:, p * PANEL + k * B : p * PANEL + (k + 1) * B] for p in range(4)])
+        terms = jnp.broadcast_to(terms, (8, B))
+        strip_cols[col, :, OFFSETS[k] : OFFSETS[k] + B] = total[:, OFFSETS[k] : OFFSETS[k] + B] + jnp.where(
+            lane == strip_at + sub, terms, 0.0)
+        if k < 3:
+            strip_cols[col, :, OFFSETS[k] + B : OFFSETS[k + 1]] = total[:, OFFSETS[k] + B : OFFSETS[k + 1]]
+    spreads = []
+    for i, step in enumerate(COL_STEPS):
+        spreads.append(send(strip_cols.at[col], strip_cols.at[col], dcol_s.at[i], dcol_r.at[i], at_col(step)))
+
+    for copy in gathers:
+        copy.wait_recv()
+    panel_t[...] = panel[...].T
+
+    for copy in spreads:
+        copy.wait_recv()
+    d_ref[strip_rows, :] = choose(owner, [strip_cols[c] for c in range(COLS)])
+    dgathers = []
+    for i, step in enumerate(CHIP_STEPS):
+        dgathers.append(send(d_ref.at[strip_rows], d_ref.at[strip_rows], dag_s.at[i], dag_r.at[i], at_chip(step)))
+
+    swaps, sums = {}, []
+    steps = CHIP_STEPS + [0]
+
+    def merge(i):
+        swaps[i].wait_recv()
+        part[i] += other_in[i]
+        if steps[i]:
+            sums.append(send(part.at[i], landed.at[i], rs_s.at[i], rs_r.at[i], at_chip(steps[i])))
+
+    for i, step in enumerate(steps):
+        peer = chip_peer(chip, step)
+        both = dot(panel_t[...], b_ref[:, pl.ds(pl.multiple_of(peer * 2 * SHARE, 2 * SHARE), 2 * SHARE)])
+        first, second = both[:, :SHARE], both[:, SHARE:]
+        part[i] = jnp.where(core == 0, first, second)
+        other[i] = jnp.where(core == 0, second, first)
+        swaps[i] = send(other.at[i], other_in.at[i], core_s.at[i], core_r.at[i], sibling)
+        if i >= 2:
+            merge(i - 2)
+    merge(len(steps) - 2)
+    merge(len(steps) - 1)
+
+    for copy in dgathers:
+        copy.wait_recv()
+    dswap = send(d_ref.at[half], d_ref.at[half], dsib_s, dsib_r, sibling)
+    dswap.wait_recv()
+
+    first_row = col * WIDTH + grp * SHARE - panel_ref[0] * PANEL
+    terms = jnp.broadcast_to(
+        shift_ref[:, pl.ds(pl.multiple_of(grp * SHARE, SHARE), SHARE)], (PANEL, SHARE))
+    on_diag = first_row + lax.broadcasted_iota(jnp.int32, (PANEL, SHARE), 1) == lax.broadcasted_iota(
+        jnp.int32, (PANEL, SHARE), 0)
+    mine = part[len(steps) - 1] + jnp.where(on_diag, terms, 0.0)
+    for i, copy in enumerate(sums):
+        copy.wait_recv()
+        mine += landed[i]
+    t_ref[...] = mine
+    for copy in sends:
+        copy.wait_send()
+
+
+def gathered(constraint_rows, shift, group_rows, panel_index):
+    f32 = jnp.float32
+    dma = pltpu.SemaphoreType.DMA
+    vmem = pl.BlockSpec(memory_space=pltpu.VMEM)
+    smem = pl.BlockSpec(memory_space=pltpu.SMEM)
+    many = lambda n: [dma((n,)), dma((n,))]
+    return pl.pallas_call(
+        gather_kernel,
+        out_shape=(jax.ShapeDtypeStruct((B, PACKED), f32), jax.ShapeDtypeStruct((PANEL, SHARE), f32)),
+        in_specs=[smem, smem, vmem, vmem],
+        out_specs=(vmem, vmem),
+        scratch_shapes=[
+            pltpu.VMEM((GROUP_ROWS, PANEL), f32),
+            pltpu.VMEM((COLS, PIECE, PANEL), f32),
+            pltpu.VMEM((GROUP_ROWS, PANEL), f32),
+            pltpu.VMEM((PANEL, GROUP_ROWS), f32),
+            pltpu.VMEM((B, PACKED), f32),
+            pltpu.VMEM((64, PACKED), f32),
+            pltpu.VMEM((7, 8, PACKED), f32),
+            pltpu.VMEM((COLS, 8, PACKED), f32),
+            pltpu.VMEM((8, PANEL, SHARE), f32),
+            pltpu.VMEM((8, PANEL, SHARE), f32),
+            pltpu.VMEM((8, PANEL, SHARE), f32),
+            pltpu.VMEM((7, PANEL, SHARE), f32),
+            *many(7), *many(7), dma, dma, *many(7), *many(7), *many(7), dma, dma, *many(8), *many(7),
+        ],
+        compiler_params=pltpu.CompilerParams(collective_id=0, has_side_effects=True, vmem_limit_bytes=40 << 20),
+    )(group_rows, panel_index, constraint_rows, shift.reshape(1, -1))
 
 
 def on_device(constraint_rows, shift, group_rows, panel_index):
-    width = constraint_rows.shape[1]
-    groups = lax.axis_size("grp")
-    col_idx = lax.axis_index("col")
-    grp_idx = lax.axis_index("grp")
-    share = width // groups
-    start = panel_index[0] * PANEL
-    owner = start // width
-    local = start - owner * width
-    live_count = lax.dynamic_index_in_dim(group_rows, grp_idx, keepdims=False)
-    row_ids = jnp.arange(constraint_rows.shape[0], dtype=jnp.int32)
-    masked = jnp.where(
-        (row_ids < live_count)[:, None], constraint_rows, jnp.zeros_like(constraint_rows)
-    )
-    own_cols = lax.dynamic_slice_in_dim(masked, local, PANEL, 1)
-    panel_cols = picked(own_cols, "col", owner)
-    mine = sent_and_summed(gram_rows(masked, panel_cols), "grp", 0)
-    shift_part = lax.dynamic_slice_in_dim(shift, grp_idx * share, share, 0)
-    mine = add_shift(mine, shift_part, col_idx * width + grp_idx * share, start)
-    from_owner = picked(mine, "col", owner)
-    owner_shard = lax.all_gather(from_owner, "grp", axis=0, tiled=True)
-    block = lax.dynamic_slice_in_dim(owner_shard, local, PANEL, 0)
-    return solve(block, mine.T)
+    d, t = gathered(constraint_rows, shift, group_rows, panel_index)
+    return solve(d, t)
 
 
 def solution(mesh):

time: 275 us -> 89 us (0.32)
  waiting for transfers between devices: 206 us -> 0 us
  Pallas kernels: 26.8 us -> 85.2 us
  between operations: 13.9 us -> 0.67 us
  other arithmetic: 7.71 us -> 0 us
  matrix products: 6.01 us -> 0 us
  starting transfers between devices: 5.79 us -> 0 us
  local copies, waits for them, and re-layouts: 7.89 us -> 2.94 us
    all_gather x3 -> x0, waiting for transfers between devices: 158 us -> none  [the longest x2 122 us: picked(): lax.all_gather(x, axis)]
    pallas_call x0 -> x1, Pallas kernels: none -> 58.3 us  [gathered(): pl.pallas_call(gather_kernel, out_shape=(jax.ShapeDtypeStruct((B, PACKED)...]
    all_to_all x1 -> x0, waiting for transfers between devices: 48.9 us -> none  [sent_and_summed(): lax.all_to_all(pieces, axis, split_axis=0, concat_axis=0, tiled=True)]
    dot_general x1 -> x0, matrix products: 6.01 us -> none  [product(): lax.dot_general(left, right, (((0,), (0,)), ((), ())), precision=lax.Prec...]
    dynamic_slice x5 -> x0, local copies, waits for them, and re-layouts: 5.84 us -> none  [the longest x1 1.67 us: picked(): lax.dynamic_index_in_dim(lax.all_gather(x, axis), root, 0, keepdims=False)]
    all_to_all x1 -> x0, starting transfers between devices: 5.53 us -> none  [sent_and_summed(): lax.all_to_all(pieces, axis, split_axis=0, concat_axis=0, tiled=True)]
    unnamed x2 -> x6, local copies, waits for them, and re-layouts: 0.01 us -> 2.94 us
  transfers between devices with their start and end apart: 4 -> 0, of which waited for: 4 -> 0; matrix products, arithmetic and copies ran while one was open for 2% -> 0% of each run, Pallas kernels for 0% -> 0%
where the time goes in v2:
time: 89 us; the launch traced here: 88.8 us
  Pallas kernels  85.2 us (96%)
  local copies, waits for them, and re-layouts  2.94 us (3%)
    pallas_call x1, Pallas kernels, gathered(): pl.pallas_call(gather_kernel, out_shape=(jax.ShapeDtypeStruct((B, PACKED)...  58.3 us
    pallas_call x1, Pallas kernels, solve(): pl.pallas_call(solve_kernel, out_shape=jax.ShapeDtypeStruct((w, n), jnp.f...  26.8 us
    unnamed x6, local copies, waits for them, and re-layouts  2.94 us

profile of v2, /device:TPU:1, one launch (start us, length us, event | category | flops | bytes accessed | tf_op | source)
XLA Modules:
  0.0 88.8 jit_solution(958353910214520553)
XLA Ops:
  0.7 0.0 copy-start
  0.7 1.6 %copy-done = f32[256,2048]{1,0:T(8,128)S(1)} copy-done((f32[256,2048]{1,0:T(8,128)S(1)}, f32[256,2048]{1,0:T(8,128)}, u32[]{:S(2)}) %copy-start) | copy-done | bytes 2097176
  2.2 0.0 copy-start.1
  2.2 0.7 copy-done.1
  2.9 0.0 copy-start.2
  2.9 0.7 copy-done.2
  3.6 58.3 %shard_map.46 = (f32[128,1280]{1,0:T(8,128)S(1)}, f32[512,128]{1,0:T(8,128)S(1)}) custom-call(s32[16]{0:T(128)S(1)} %copy-done.2, s32[1]{0:T(128)S(6)} %copy.5.panel_ref, f32[256,2048]{1,0:T(8,128)S(1)} %copy-done, f32[1,2048]{1,0:T(1,128)S(1)} %bitcast.1), custom_call_target="tpu_custom_call" | custom-call | tf_op jit(solution)/shard_map/pallas_call | solution.py:285
  61.9 26.8 %shard_map.47 = f32[128,512]{1,0:T(8,128)} custom-call(f32[128,1280]{1,0:T(8,128)S(1)} %get-tuple-element.7.d_ref, f32[512,128]{1,0:T(8,128)S(1)} %get-tuple-element.8.t_ref), custom_call_target="tpu_custom_call" | custom-call | tf_op jit(solution)/shard_map/pallas_call | solution.py:90
Async XLA Ops:
  0.7 1.6 %copy-start = (f32[256,2048]{1,0:T(8,128)S(1)}, f32[256,2048]{1,0:T(8,128)}, u32[]{:S(2)}) copy-start(f32[256,2048]{1,0:T(8,128)} %b_ref.1) | copy-start | bytes 6291460
  2.2 0.7 copy-start.1
  2.9 0.7 copy-start.2

commit v3 on v2

--- a/solution.py
+++ b/solution.py
@@ -58,43 +58,6 @@
     return lax.dot_general(a, b, (dims, ((), ())), precision=HI, preferred_element_type=jnp.float32)
 
 
-def factor_and_solve(m_ref, blocks):
-    n = blocks * B
-    width = m_ref.shape[1]
-    for k in range(blocks):
-        at = k * B
-        w = jnp.concatenate(inv_chol([m_ref[at + 8 * i : at + 8 * i + 8, at : at + B] for i in range(16)]), axis=0)
-        u = dot(w, m_ref[at : at + B, at + B :])
-        if k == blocks - 1:
-            return u
-        m_ref[at : at + B, at + B :] = u
-        for r in range(k + 1, blocks):
-            left = u[:, (r - k - 1) * B : (r - k) * B]
-            m_ref[r * B : (r + 1) * B, r * B :] -= dot(left, u[:, (r - k - 1) * B :], ((0,), (0,)))
-
-
-def solve_kernel(d_ref, t_ref, x_ref, m_ref):
-    n, w = t_ref.shape
-    blocks = n // B
-    for k in range(blocks):
-        m_ref[k * B : (k + 1) * B, k * B : n] = d_ref[:, OFFSETS[k] : OFFSETS[k] + n - k * B]
-    m_ref[:, n:] = t_ref[...]
-    last = factor_and_solve(m_ref, blocks)
-    for k in range(blocks):
-        block = last if k == blocks - 1 else m_ref[k * B : (k + 1) * B, n:]
-        x_ref[:, k * B : (k + 1) * B] = block.T
-
-
-def solve(d, t):
-    n, w = t.shape
-    return pl.pallas_call(
-        solve_kernel,
-        out_shape=jax.ShapeDtypeStruct((w, n), jnp.float32),
-        scratch_shapes=[pltpu.VMEM((n, n + w), jnp.float32)],
-        compiler_params=pltpu.CompilerParams(vmem_limit_bytes=32 << 20),
-    )(d, t)
-
-
 GROUP_ROWS = 256
 WIDTH = 2048
 PANEL = 512
@@ -135,9 +98,9 @@
 COL_STEPS = [6, 2, 5, 7, 1, 3, 4]
 
 
-def gather_kernel(
-    groups_ref, panel_ref, b_ref, shift_ref, d_ref, t_ref,
-    own, scat, panel, panel_t, pack, pack_in, strips, strip_cols, part, other, other_in, landed,
+def panel_kernel(
+    groups_ref, panel_ref, b_ref, shift_ref, x_ref,
+    d_ref, m_ref, t_ref, own, scat, panel, panel_t, pack, pack_in, strips, strip_cols, part, other, other_in, landed,
     scat_s, scat_r, ag_s, ag_r, dcore_s, dcore_r, drs_s, drs_r, dcol_s, dcol_r, dag_s, dag_r, dsib_s, dsib_r,
     core_s, core_r, rs_s, rs_r,
 ):
@@ -262,32 +225,60 @@
     dswap = send(d_ref.at[half], d_ref.at[half], dsib_s, dsib_r, sibling)
     dswap.wait_recv()
 
-    first_row = col * WIDTH + grp * SHARE - panel_ref[0] * PANEL
-    terms = jnp.broadcast_to(
-        shift_ref[:, pl.ds(pl.multiple_of(grp * SHARE, SHARE), SHARE)], (PANEL, SHARE))
-    on_diag = first_row + lax.broadcasted_iota(jnp.int32, (PANEL, SHARE), 1) == lax.broadcasted_iota(
-        jnp.int32, (PANEL, SHARE), 0)
-    mine = part[len(steps) - 1] + jnp.where(on_diag, terms, 0.0)
-    for i, copy in enumerate(sums):
-        copy.wait_recv()
-        mine += landed[i]
-    t_ref[...] = mine
+    def sum_rows():
+        first_row = col * WIDTH + grp * SHARE - panel_ref[0] * PANEL
+        terms = jnp.broadcast_to(
+            shift_ref[:, pl.ds(pl.multiple_of(grp * SHARE, SHARE), SHARE)], (PANEL, SHARE))
+        on_diag = first_row + lax.broadcasted_iota(jnp.int32, (PANEL, SHARE), 1) == lax.broadcasted_iota(
+            jnp.int32, (PANEL, SHARE), 0)
+        mine = part[len(steps) - 1] + jnp.where(on_diag, terms, 0.0)
+        for i, copy in enumerate(sums):
+            copy.wait_recv()
+            mine += landed[i]
+        t_ref[...] = mine
+
+    for k in range(4):
+        m_ref[k * B : (k + 1) * B, k * B :] = d_ref[:, OFFSETS[k] : OFFSETS[k] + PANEL - k * B]
+    inverses, uppers = [], []
+    for k in range(4):
+        if k == 3:
+            sum_rows()
+        at = k * B
+        tiles = [m_ref[at + 8 * i : at + 8 * i + 8, at : at + B] for i in range(16)]
+        w = jnp.concatenate(inv_chol(tiles), axis=0)
+        inverses.append(w)
+        if k == 3:
+            break
+        u = dot(w, m_ref[at : at + B, at + B :])
+        uppers.append(u)
+        for r in range(k + 1, 4):
+            left = u[:, (r - k - 1) * B : (r - k) * B]
+            m_ref[r * B : (r + 1) * B, r * B :] -= dot(left, u[:, (r - k - 1) * B :], ((0,), (0,)))
+    rest = [t_ref[k * B : (k + 1) * B, :] for k in range(4)]
+    for k in range(4):
+        x = dot(inverses[k], rest[k])
+        x_ref[:, k * B : (k + 1) * B] = x.T
+        for r in range(k + 1, 4):
+            rest[r] = rest[r] - dot(uppers[k][:, (r - k - 1) * B : (r - k) * B], x, ((0,), (0,)))
     for copy in sends:
         copy.wait_send()
 
 
-def gathered(constraint_rows, shift, group_rows, panel_index):
+def panel_rows(constraint_rows, shift, group_rows, panel_index):
     f32 = jnp.float32
     dma = pltpu.SemaphoreType.DMA
     vmem = pl.BlockSpec(memory_space=pltpu.VMEM)
     smem = pl.BlockSpec(memory_space=pltpu.SMEM)
     many = lambda n: [dma((n,)), dma((n,))]
     return pl.pallas_call(
-        gather_kernel,
-        out_shape=(jax.ShapeDtypeStruct((B, PACKED), f32), jax.ShapeDtypeStruct((PANEL, SHARE), f32)),
+        panel_kernel,
+        out_shape=jax.ShapeDtypeStruct((SHARE, PANEL), f32),
         in_specs=[smem, smem, vmem, vmem],
-        out_specs=(vmem, vmem),
+        out_specs=vmem,
         scratch_shapes=[
+            pltpu.VMEM((B, PACKED), f32),
+            pltpu.VMEM((PANEL, PANEL), f32),
+            pltpu.VMEM((PANEL, SHARE), f32),
             pltpu.VMEM((GROUP_ROWS, PANEL), f32),
             pltpu.VMEM((COLS, PIECE, PANEL), f32),
             pltpu.VMEM((GROUP_ROWS, PANEL), f32),
@@ -307,8 +298,7 @@
 
 
 def on_device(constraint_rows, shift, group_rows, panel_index):
-    d, t = gathered(constraint_rows, shift, group_rows, panel_index)
-    return solve(d, t)
+    return panel_rows(constraint_rows, shift, group_rows, panel_index)
 
 
 def solution(mesh):

time: 89 us -> 71.3 us (0.80)
  Pallas kernels: 85.2 us -> 66.8 us
    pallas_call x2 -> x1, Pallas kernels: 85.2 us -> 66.8 us  [panel_rows(): pl.pallas_call(panel_kernel, out_shape=jax.ShapeDtypeStruct((SHARE, PANEL...]
    unnamed x6 -> x7, local copies, waits for them, and re-layouts: 2.94 us -> 3.64 us
where the time goes in v3:
time: 71.3 us; the launch traced here: 71.1 us
  Pallas kernels  66.8 us (94%)
  local copies, waits for them, and re-layouts  3.64 us (5%)
    pallas_call x1, Pallas kernels, panel_rows(): pl.pallas_call(panel_kernel, out_shape=jax.ShapeDtypeStruct((SHARE, PANEL...  66.8 us
    unnamed x7, local copies, waits for them, and re-layouts  3.64 us

profile of v3, /device:TPU:1, one launch (start us, length us, event | category | flops | bytes accessed | tf_op | source)
XLA Modules:
  0.0 71.1 jit_solution(1605385311310393757)
XLA Ops:
  0.7 0.0 copy-start
  0.7 1.6 %copy-done = f32[256,2048]{1,0:T(8,128)S(1)} copy-done((f32[256,2048]{1,0:T(8,128)S(1)}, f32[256,2048]{1,0:T(8,128)}, u32[]{:S(2)}) %copy-start) | copy-done | bytes 2097176
  2.2 0.0 copy-start.1
  2.2 0.7 copy-done.1
  2.9 0.0 copy-start.2
  2.9 0.7 copy-done.2
  3.6 66.8 %shard_map.46 = f32[128,512]{1,0:T(8,128)S(1)} custom-call(s32[16]{0:T(128)S(1)} %copy-done.2, s32[1]{0:T(128)S(6)} %copy.6.panel_ref, f32[256,2048]{1,0:T(8,128)S(1)} %copy-done, f32[1,2048]{1,0:T(1,128)S(1)} %bitcast.1), custom_call_target="tpu_custom_call" | custom-call | tf_op jit(solution)/shard_map/pallas_call | solution.py:273
  70.4 0.7 copy.7
Async XLA Ops:
  0.7 1.6 %copy-start = (f32[256,2048]{1,0:T(8,128)S(1)}, f32[256,2048]{1,0:T(8,128)}, u32[]{:S(2)}) copy-start(f32[256,2048]{1,0:T(8,128)} %b_ref.1) | copy-start | bytes 6291460
  2.2 0.7 copy-start.1
  2.9 0.7 copy-start.2

commit v4 on v3

v4 whole, which is shorter than its diff:
```python
import jax, jax.numpy as jnp
from jax import lax
from jax.experimental import pallas as pl
from jax.experimental.pallas import tpu as pltpu
from jax.sharding import PartitionSpec as P

B = 128
HI = lax.Precision.HIGHEST


def inv_chol(rows):
    lane = lax.broadcasted_iota(jnp.int32, (8, B), 1)
    rows = list(rows)
    for s in range(16):
        k0 = 8 * s
        inside = (lane >= k0) & (lane < k0 + 8)
        tile = rows[s]
        spread = lambda t, l: jnp.broadcast_to(t[:, k0 + l : k0 + l + 1], (8, B))
        cols = [spread(tile, l) for l in range(8)]
        c = {(m, l): jnp.broadcast_to(cols[l][m : m + 1, :], (8, B)) for l in range(8) for m in range(l, 8)}
        r = [
            jnp.where(inside, jnp.where(lane == k0 + m, 1.0, 0.0), jnp.broadcast_to(tile[m : m + 1, :], (8, B)))
            for m in range(8)
        ]
        rs, low = {}, {}
        fs = [[spread(rows[i], l) for l in range(8)] for i in range(s + 1, min(s + 3, 16))]
        for j in range(8):
            rs[j] = lax.rsqrt(c[j, j])
            r[j] = r[j] * rs[j]
            for m in range(j + 1, 8):
                low[m, j] = c[m, j] * rs[j]
            for m in range(j + 1, 8):
                for n in range(j + 1, m + 1):
                    c[m, n] = c[m, n] - low[m, j] * low[n, j]
                r[m] = r[m] - low[m, j] * r[j]
        sub = lax.broadcasted_iota(jnp.int32, (8, B), 0)
        done = r[0]
        for j in range(1, 8):
            done = jnp.where(sub == j, r[j], done)
        rows[s] = jnp.where(lane < k0 + 8, done, 0.0)
        if s < 15:
            h = done.astype(jnp.bfloat16).astype(jnp.float32)
            mid = (done - h).astype(jnp.bfloat16).astype(jnp.float32)
            tail = done - h - mid
            lhs = jnp.concatenate([h, h, mid, h, tail, mid], axis=0).astype(jnp.bfloat16)
            rhs = jnp.concatenate([h, mid, h, tail, h, mid], axis=0).astype(jnp.bfloat16)
            late = lax.dot_general(lhs, rhs, (((0,), (0,)), ((), ())), preferred_element_type=jnp.float32)
            for i in range(s + 3, 16):
                rows[i] = jnp.where(inside, 0.0, rows[i]) - late[8 * i : 8 * i + 8, :]
            for d in range(2):
                if s + 1 + d < 16:
                    f = fs[d]
                    for j in range(8):
                        f[j] = f[j] * rs[j]
                        for m in range(j + 1, 8):
                            f[m] = f[m] - low[m, j] * f[j]
                    p0 = f[0] * r[0] + f[1] * r[1]
                    p1 = f[2] * r[2] + f[3] * r[3]
                    p2 = f[4] * r[4] + f[5] * r[5]
                    p3 = f[6] * r[6] + f[7] * r[7]
                    rows[s + 1 + d] = jnp.where(inside, 0.0, rows[s + 1 + d]) - ((p0 + p1) + (p2 + p3))
    return rows


def dot(a, b, dims=((1,), (0,))):
    return lax.dot_general(a, b, (dims, ((), ())), precision=HI, preferred_element_type=jnp.float32)


GROUP_ROWS = 256
WIDTH = 2048
PANEL = 512
CHIPS = 8
RING = 4
PIECE = GROUP_ROWS // RING
HALF = PANEL // 2
SHARE = 128
OFFSETS = [0, 512, 896, 1152]
PACKED = 1280
MESH = pl.DeviceIdType.MESH
AROUND = [2, 1, 3]
LAG = 4


def choose(index, arrays):
    chosen = arrays[0]
    for i in range(1, len(arrays)):
        chosen = jnp.where(index == i, arrays[i], chosen)
    return chosen


def panel_kernel(
    groups_hbm, panel_hbm, b_hbm, shift_hbm, x_ref,
    groups_ref, panel_ref, b_ref, shift_ref, d_ref, m_ref, own, scat, cross, panel, panel_t,
    pack, pack_in, strips, strip_y, strip_x, part, other, other_in, first_x, first_z, last_z, last_x,
    load_s, scat_s, scat_r, cross_s, cross_r, ag_s, ag_r, dcore_s, dcore_r, drs_s, drs_r, dy_s, dy_r, dx_s, dx_r,
    dag_s, dag_r, dsib_s, dsib_r, core_s, core_r, fx_s, fx_r, fz_s, fz_r, lz_s, lz_r, lx_s, lx_r,
):
    grp, col = lax.axis_index("grp"), lax.axis_index("col")
    z, x, core = grp // 4, lax.rem(grp // 2, 2), lax.rem(grp, 2)
    x_hi, y = col // RING, lax.rem(col, RING)

    def chip_of(dz, dx):
        return lax.rem(z + dz, RING) * 2 + lax.rem(x + dx, 2)

    def at_chip(dz, dx):
        return {"grp": chip_of(dz, dx) * 2 + core}

    def y_of(dy):
        return lax.rem(y + dy, RING)

    def at_y(dy):
        return {"col": x_hi * RING + y_of(dy)}

    sibling = {"grp": grp + 1 - 2 * core}
    across = {"col": (1 - x_hi) * RING + y}
    other_chips = [(dz, dx) for dx in (1, 0) for dz in AROUND + [0] if dz or dx]

    loads = [
        pltpu.make_async_copy(src, dst, load_s.at[i])
        for i, (src, dst) in enumerate(
            [(b_hbm, b_ref), (groups_hbm, groups_ref), (panel_hbm, panel_ref), (shift_hbm, shift_ref)])
    ]
    for copy in loads:
        copy.start()

    barrier = pltpu.get_barrier_semaphore()
    peers = [sibling, across] + [at_y(dy) for dy in AROUND] + [at_chip(*step) for step in other_chips]
    for peer in peers:
        pl.semaphore_signal(barrier, 1, device_id=peer, device_id_type=MESH)

    sends = []

    def send(src, dst, s, r, to):
        copy = pltpu.make_async_remote_copy(
            src_ref=src, dst_ref=dst, send_sem=s, recv_sem=r, device_id=to, device_id_type=MESH
        )
        copy.start()
        sends.append(copy)
        return copy

    def arrived(copies):
        for copy in copies:
            copy.wait_recv()

    for copy in loads[1:] + loads[:1]:
        copy.wait()
    owner = panel_ref[0] // 4
    owner_x, owner_y = owner // RING, lax.rem(owner, RING)
    local = lax.rem(panel_ref[0], 4)
    live = groups_ref[grp]
    row = lax.broadcasted_iota(jnp.int32, (GROUP_ROWS, PANEL), 0)
    own[...] = jnp.where(row < live, choose(local, [b_ref[:, k * PANEL : (k + 1) * PANEL] for k in range(4)]), 0.0)

    for k in range(4):
        pack[:, OFFSETS[k] : OFFSETS[k] + PANEL - k * B] = dot(
            own[:, k * B : (k + 1) * B], own[:, k * B :], ((0,), (0,)))
    pl.semaphore_wait(barrier, len(peers))

    half = pl.ds(pl.multiple_of(core * 64, 64), 64)
    half_other = pl.ds(pl.multiple_of((1 - core) * 64, 64), 64)
    swap = send(pack.at[half_other], pack_in, dcore_s, dcore_r, sibling)

    piece = pl.ds(pl.multiple_of(y * PIECE, PIECE), PIECE)
    columns = [pl.ds(h * HALF, HALF) for h in range(2)]
    scatters = [
        [
            send(own.at[pl.ds(pl.multiple_of(y_of(dy) * PIECE, PIECE), PIECE), columns[h]], scat.at[h, y],
                 scat_s.at[h, i], scat_r.at[h, i], at_y(dy))
            for i, dy in enumerate(AROUND)
        ]
        for h in range(2)
    ]
    for h in range(2):
        scat[h, y] = own[piece, h * HALF : (h + 1) * HALF]

    swap.wait_recv()
    pack[half, :] += pack_in[...]
    reduces = [
        send(pack.at[pl.ds(pl.multiple_of(core * 64 + chip_of(*step) * 8, 8), 8)], strips.at[i],
             drs_s.at[i], drs_r.at[i], at_chip(*step))
        for i, step in enumerate(other_chips)
    ]

    def pass_across(h):
        arrived(scatters[h])
        cross[h, x_hi] = choose(owner_y, [scat[h, i] for i in range(RING)])
        return send(cross.at[h, x_hi], cross.at[h, x_hi], cross_s.at[h], cross_r.at[h], across)

    def gather(h):
        crossings[h].wait_recv()
        panel[piece, h * HALF : (h + 1) * HALF] = choose(owner_x, [cross[h, i] for i in range(2)])
        return [
            send(panel.at[piece, columns[h]], panel.at[piece, columns[h]], ag_s.at[h, i], ag_r.at[h, i], at_y(dy))
            for i, dy in enumerate(AROUND)
        ]

    crossings = [pass_across(0)]

    strip_at = pl.multiple_of(core * 64 + (z * 2 + x) * 8, 8)
    strip_rows = pl.ds(strip_at, 8)
    total = pack[strip_rows, :]
    for i, copy in enumerate(reduces):
        copy.wait_recv()
        total += strips[i]
    lane = lax.broadcasted_iota(jnp.int32, (8, B), 1)
    sub = lax.broadcasted_iota(jnp.int32, (8, B), 0)
    for k in range(4):
        terms = choose(local, [shift_ref[:, p * PANEL + k * B : p * PANEL + (k + 1) * B] for p in range(4)])
        terms = jnp.broadcast_to(terms, (8, B))
        strip_y[y, :, OFFSETS[k] : OFFSETS[k] + B] = total[:, OFFSETS[k] : OFFSETS[k] + B] + jnp.where(
            lane == strip_at + sub, terms, 0.0)
        if k < 3:
            strip_y[y, :, OFFSETS[k] + B : OFFSETS[k + 1]] = total[:, OFFSETS[k] + B : OFFSETS[k + 1]]
    spreads = [
        send(strip_y.at[y], strip_y.at[y], dy_s.at[i], dy_r.at[i], at_y(dy)) for i, dy in enumerate(AROUND)
    ]

    crossings.append(pass_across(1))
    gathers = [gather(0)]
    gathers.append(gather(1))

    arrived(spreads)
    strip_x[x_hi] = choose(owner_y, [strip_y[i] for i in range(RING)])
    strip_cross = send(strip_x.at[x_hi], strip_x.at[x_hi], dx_s, dx_r, across)

    swaps, to_x, to_z = {}, {}, {}

    def gram(h, dz, dx):
        at = pl.multiple_of(chip_of(dz, dx) * 2 * SHARE, 2 * SHARE)
        both = dot(panel_t[h * HALF : (h + 1) * HALF, :], b_ref[:, pl.ds(at, 2 * SHARE)])
        first, second = both[:, :SHARE], both[:, SHARE:]
        part[h, dz, dx] = jnp.where(core == 0, first, second)
        other[h, dz, dx] = jnp.where(core == 0, second, first)
        swaps[h, dz, dx] = send(
            other.at[h, dz, dx], other_in.at[h, dz, dx], core_s.at[h, dz, dx], core_r.at[h, dz, dx], sibling)

    def merge(h, dz, dx):
        swaps[h, dz, dx].wait_recv()
        part[h, dz, dx] += other_in[h, dz, dx]
        if h == 0 and dx == 1:
            to_x[dz] = send(part.at[0, dz, 1], first_x.at[dz], fx_s.at[dz], fx_r.at[dz], at_chip(0, 1))
        if h == 1 and dx == 0 and dz:
            to_z[dz] = send(part.at[1, dz], last_z.at[dz], lz_s.at[dz], lz_r.at[dz], at_chip(dz, 0))

    def pass_on_z(dz):
        to_x[dz].wait_recv()
        part[0, dz, 0] += first_x[dz]
        if dz:
            from_z.append(send(part.at[0, dz, 0], first_z.at[dz], fz_s.at[dz], fz_r.at[dz], at_chip(dz, 0)))

    def pass_on_x():
        for dz in AROUND:
            to_z[dz].wait_recv()
            part[1, 0] += last_z[dz]
        return send(part.at[1, 0, 1], last_x, lx_s, lx_r, at_chip(0, 1))

    from_z = []
    order = [(h, dz, dx) for h in range(2) for dz, dx in (
        [(dz, dx) for dx in (1, 0) for dz in AROUND + [0]] if h == 0
        else [(dz, dx) for dz in AROUND + [0] for dx in (1, 0)])]
    for i, step in enumerate(order):
        h = step[0]
        if i == 8 * h:
            arrived(gathers[h])
            panel_t[h * HALF : (h + 1) * HALF, :] = panel[:, h * HALF : (h + 1) * HALF].T
        gram(*step)
        if i == LAG:
            strip_cross.wait_recv()
            d_ref[strip_rows, :] = choose(owner_x, [strip_x[c] for c in range(2)])
            dgathers = [
                send(d_ref.at[strip_rows], d_ref.at[strip_rows], dag_s.at[c], dag_r.at[c], at_chip(*chip))
                for c, chip in enumerate(other_chips)
            ]
        if i >= LAG:
            merge(*order[i - LAG])
    for step in order[-LAG:]:
        merge(*step)
    arrived(dgathers)
    dswap = send(d_ref.at[half], d_ref.at[half], dsib_s, dsib_r, sibling)
    pass_on_z(2)
    dswap.wait_recv()

    first_row = col * WIDTH + grp * SHARE - panel_ref[0] * PANEL
    terms = jnp.broadcast_to(shift_ref[:, pl.ds(pl.multiple_of(grp * SHARE, SHARE), SHARE)], (HALF, SHARE))

    def rows(h, total):
        at_row = h * HALF + lax.broadcasted_iota(jnp.int32, (HALF, SHARE), 0)
        on_diag = first_row + lax.broadcasted_iota(jnp.int32, (HALF, SHARE), 1) == at_row
        total = part[h, 0, 0] + jnp.where(on_diag, terms, 0.0) + total
        return [total[:B, :], total[B:, :]]

    def solved(k, right):
        x_k = dot(inverses[k], right)
        x_ref[:, k * B : (k + 1) * B] = x_k.T
        return x_k

    def under(k, left, right):
        return dot(uppers[k][:, left * B : right * B], x_rows[k], ((0,), (0,)))

    for k in range(4):
        m_ref[k * B : (k + 1) * B, k * B :] = d_ref[:, OFFSETS[k] : OFFSETS[k] + PANEL - k * B]
    inverses, uppers = [], []
    for k in range(4):
        if k == 1:
            pass_on_z(1)
            pass_on_z(3)
        if k == 2:
            pass_on_z(0)
            from_x = pass_on_x()
        if k == 3:
            arrived(from_z)
            upper_rows = rows(0, first_z[1] + first_z[2] + first_z[3])
            x_rows = [solved(0, upper_rows[0])]
            x_rows.append(solved(1, upper_rows[1] - under(0, 0, 1)))
            carried = under(0, 1, 3) + under(1, 0, 2)
        at = k * B
        tiles = [m_ref[at + 8 * i : at + 8 * i + 8, at : at + B] for i in range(16)]
        w = jnp.concatenate(inv_chol(tiles), axis=0)
        inverses.append(w)
        if k == 3:
            break
        u = dot(w, m_ref[at : at + B, at + B :])
        uppers.append(u)
        for r in range(k + 1, 4):
            left = u[:, (r - k - 1) * B : (r - k) * B]
            m_ref[r * B : (r + 1) * B, r * B :] -= dot(left, u[:, (r - k - 1) * B :], ((0,), (0,)))
    from_x.wait_recv()
    lower_rows = rows(1, last_x[...])
    x_rows.append(solved(2, lower_rows[0] - carried[:B, :]))
    solved(3, lower_rows[1] - carried[B:, :] - under(2, 0, 1))
    for copy in sends:
        copy.wait_send()


def panel_rows(constraint_rows, shift, group_rows, panel_index):
    f32 = jnp.float32
    dma = pltpu.SemaphoreType.DMA
    buf = lambda *shape: pltpu.VMEM(shape, f32)
    pair = lambda *shape: [dma(*shape) if shape else dma] * 2
    return pl.pallas_call(
        panel_kernel,
        out_shape=jax.ShapeDtypeStruct((SHARE, PANEL), f32),
        in_specs=[pl.BlockSpec(memory_space=pl.ANY)] * 4,
        out_specs=pl.BlockSpec(memory_space=pltpu.VMEM),
        scratch_shapes=[
            pltpu.SMEM((16,), jnp.int32),
            pltpu.SMEM((1,), jnp.int32),
            buf(GROUP_ROWS, WIDTH),
            buf(1, WIDTH),
            buf(B, PACKED),
            buf(PANEL, PANEL),
            buf(GROUP_ROWS, PANEL),
            buf(2, RING, PIECE, HALF),
            buf(2, 2, PIECE, HALF),
            buf(GROUP_ROWS, PANEL),
            buf(PANEL, GROUP_ROWS),
            buf(B, PACKED),
            buf(64, PACKED),
            buf(7, 8, PACKED),
            buf(RING, 8, PACKED),
            buf(2, 8, PACKED),
            *[buf(2, RING, 2, HALF, SHARE)] * 3,
            buf(RING, HALF, SHARE),
            buf(RING, HALF, SHARE),
            buf(RING, 2, HALF, SHARE),
            buf(HALF, SHARE),
            dma((4,)),
            *pair((2, 3)), *pair((2,)), *pair((2, 3)), *pair(), *pair((7,)), *pair((3,)), *pair(),
            *pair((7,)), *pair(), *pair((2, RING, 2)), *pair((RING,)), *pair((RING,)), *pair((RING,)), *pair(),
        ],
        compiler_params=pltpu.CompilerParams(collective_id=0, has_side_effects=True, vmem_limit_bytes=56 << 20),
    )(group_rows, panel_index, constraint_rows, shift.reshape(1, -1))


def on_device(constraint_rows, shift, group_rows, panel_index):
    return panel_rows(constraint_rows, shift, group_rows, panel_index)


def solution(mesh):
    placed = (P("grp", "col"), P("col"), P(), P())
    return jax.shard_map(
        on_device, mesh=mesh, in_specs=placed, out_specs=P(("col", "grp"), None), check_vma=False
    )
```

time: 71.3 us -> 59.8 us (0.84)
  Pallas kernels: 66.8 us -> 57.3 us
  local copies, waits for them, and re-layouts: 3.64 us -> 1.67 us
    pallas_call x1, Pallas kernels: 66.8 us -> 57.3 us  [panel_rows(): pl.pallas_call(panel_kernel, out_shape=jax.ShapeDtypeStruct((SHARE, PANEL...]
    unnamed x7 -> x1, local copies, waits for them, and re-layouts: 3.64 us -> 1.67 us
where the time goes in v4:
time: 59.8 us; the launch traced here: 59.7 us
  Pallas kernels  57.3 us (96%)
  local copies, waits for them, and re-layouts  1.67 us (3%)
  between operations  0.66 us (1%)
    pallas_call x1, Pallas kernels, panel_rows(): pl.pallas_call(panel_kernel, out_shape=jax.ShapeDtypeStruct((SHARE, PANEL...  57.3 us
    unnamed x1, local copies, waits for them, and re-layouts  1.67 us

profile of v4, /device:TPU:1, one launch (start us, length us, event | category | flops | bytes accessed | tf_op | source)
XLA Modules:
  0.0 59.7 jit_solution(10484805591050174734)
XLA Ops:
  0.7 57.3 %shard_map.46 = f32[128,512]{1,0:T(8,128)} custom-call(s32[16]{0:T(128)} %groups_hbm.1, s32[1]{0:T(128)S(6)} %copy.6.panel_hbm, f32[256,2048]{1,0:T(8,128)} %b_hbm.1, f32[1,2048]{1,0:T(1,128)} %bitcast.1), custom_call_target="tpu_custom_call" | custom-call | tf_op jit(solution)/shard_map/pallas_call | solution.py:340
  58.0 1.7 %copy.7 = f32[128,512]{1,0:T(8,128)} copy(f32[128,512]{1,0:T(8,128)} %shard_map.46) | data formatting | bytes 524288

commit v5 on v4

--- a/solution.py
+++ b/solution.py
@@ -8,11 +8,13 @@
 HI = lax.Precision.HIGHEST
 
 
-def inv_chol(rows):
+def inv_chol(rows, midway=None):
     lane = lax.broadcasted_iota(jnp.int32, (8, B), 1)
     rows = list(rows)
     for s in range(16):
         k0 = 8 * s
+        if s == 8 and midway:
+            midway()
         inside = (lane >= k0) & (lane < k0 + 8)
         tile = rows[s]
         spread = lambda t, l: jnp.broadcast_to(t[:, k0 + l : k0 + l + 1], (8, B))
@@ -78,7 +80,7 @@
 PACKED = 1280
 MESH = pl.DeviceIdType.MESH
 AROUND = [2, 1, 3]
-LAG = 4
+LAG = 2
 
 
 def choose(index, arrays):
@@ -223,62 +225,66 @@
     strip_x[x_hi] = choose(owner_y, [strip_y[i] for i in range(RING)])
     strip_cross = send(strip_x.at[x_hi], strip_x.at[x_hi], dx_s, dx_r, across)
 
+    strip_cross.wait_recv()
+    d_ref[strip_rows, :] = choose(owner_x, [strip_x[c] for c in range(2)])
+    parts = [pl.ds(0, B), pl.ds(B, PACKED - B)]
+    dgathers = [
+        [
+            send(d_ref.at[strip_rows, cols], d_ref.at[strip_rows, cols], dag_s.at[p, c], dag_r.at[p, c], at_chip(*chip))
+            for c, chip in enumerate(other_chips)
+        ]
+        for p, cols in enumerate(parts)
+    ]
+
+    def to_sibling(p):
+        arrived(dgathers[p])
+        return send(d_ref.at[half, parts[p]], d_ref.at[half, parts[p]], dsib_s.at[p], dsib_r.at[p], sibling)
+
+
     swaps, to_x, to_z = {}, {}, {}
 
-    def gram(h, dz, dx):
-        at = pl.multiple_of(chip_of(dz, dx) * 2 * SHARE, 2 * SHARE)
-        both = dot(panel_t[h * HALF : (h + 1) * HALF, :], b_ref[:, pl.ds(at, 2 * SHARE)])
-        first, second = both[:, :SHARE], both[:, SHARE:]
-        part[h, dz, dx] = jnp.where(core == 0, first, second)
-        other[h, dz, dx] = jnp.where(core == 0, second, first)
-        swaps[h, dz, dx] = send(
-            other.at[h, dz, dx], other_in.at[h, dz, dx], core_s.at[h, dz, dx], core_r.at[h, dz, dx], sibling)
-
-    def merge(h, dz, dx):
-        swaps[h, dz, dx].wait_recv()
-        part[h, dz, dx] += other_in[h, dz, dx]
-        if h == 0 and dx == 1:
-            to_x[dz] = send(part.at[0, dz, 1], first_x.at[dz], fx_s.at[dz], fx_r.at[dz], at_chip(0, 1))
-        if h == 1 and dx == 0 and dz:
-            to_z[dz] = send(part.at[1, dz], last_z.at[dz], lz_s.at[dz], lz_r.at[dz], at_chip(dz, 0))
+    def gram(h, dz):
+        at = pl.multiple_of(lax.rem(z + dz, RING) * 4 * SHARE, 4 * SHARE)
+        block = dot(panel_t[h * HALF : (h + 1) * HALF, :], b_ref[:, pl.ds(at, 4 * SHARE)])
+        for chip_x in range(2):
+            dx = lax.rem(x + chip_x, 2)
+            first, second = (block[:, (2 * chip_x + c) * SHARE : (2 * chip_x + c + 1) * SHARE] for c in range(2))
+            part[h, dz, dx] = jnp.where(core == 0, first, second)
+            other[h, dz, dx] = jnp.where(core == 0, second, first)
+        swaps[h, dz] = send(other.at[h, dz], other_in.at[h, dz], core_s.at[h, dz], core_r.at[h, dz], sibling)
+
+    def merge(h, dz):
+        swaps[h, dz].wait_recv()
+        part[h, dz] += other_in[h, dz]
+        if h == 1:
+            to_x[dz] = send(part.at[1, dz, 1], first_x.at[dz], fx_s.at[dz], fx_r.at[dz], at_chip(0, 1))
+        elif dz:
+            to_z[dz] = send(part.at[0, dz], last_z.at[dz], lz_s.at[dz], lz_r.at[dz], at_chip(dz, 0))
 
     def pass_on_z(dz):
         to_x[dz].wait_recv()
-        part[0, dz, 0] += first_x[dz]
+        part[1, dz, 0] += first_x[dz]
         if dz:
-            from_z.append(send(part.at[0, dz, 0], first_z.at[dz], fz_s.at[dz], fz_r.at[dz], at_chip(dz, 0)))
+            from_z.append(send(part.at[1, dz, 0], first_z.at[dz], fz_s.at[dz], fz_r.at[dz], at_chip(dz, 0)))
 
     def pass_on_x():
         for dz in AROUND:
             to_z[dz].wait_recv()
-            part[1, 0] += last_z[dz]
-        return send(part.at[1, 0, 1], last_x, lx_s, lx_r, at_chip(0, 1))
+            part[0, 0] += last_z[dz]
+        return send(part.at[0, 0, 1], last_x, lx_s, lx_r, at_chip(0, 1))
 
     from_z = []
-    order = [(h, dz, dx) for h in range(2) for dz, dx in (
-        [(dz, dx) for dx in (1, 0) for dz in AROUND + [0]] if h == 0
-        else [(dz, dx) for dz in AROUND + [0] for dx in (1, 0)])]
-    for i, step in enumerate(order):
-        h = step[0]
-        if i == 8 * h:
+    order = [(h, dz) for h in range(2) for dz in AROUND + [0]]
+    for i, (h, dz) in enumerate(order):
+        if i == 4 * h:
             arrived(gathers[h])
             panel_t[h * HALF : (h + 1) * HALF, :] = panel[:, h * HALF : (h + 1) * HALF].T
-        gram(*step)
-        if i == LAG:
-            strip_cross.wait_recv()
-            d_ref[strip_rows, :] = choose(owner_x, [strip_x[c] for c in range(2)])
-            dgathers = [
-                send(d_ref.at[strip_rows], d_ref.at[strip_rows], dag_s.at[c], dag_r.at[c], at_chip(*chip))
-                for c, chip in enumerate(other_chips)
-            ]
+        gram(h, dz)
         if i >= LAG:
             merge(*order[i - LAG])
     for step in order[-LAG:]:
         merge(*step)
-    arrived(dgathers)
-    dswap = send(d_ref.at[half], d_ref.at[half], dsib_s, dsib_r, sibling)
-    pass_on_z(2)
-    dswap.wait_recv()
+    to_sibling(0).wait_recv()
 
     first_row = col * WIDTH + grp * SHARE - panel_ref[0] * PANEL
     terms = jnp.broadcast_to(shift_ref[:, pl.ds(pl.multiple_of(grp * SHARE, SHARE), SHARE)], (HALF, SHARE))
@@ -297,25 +303,30 @@
     def under(k, left, right):
         return dot(uppers[k][:, left * B : right * B], x_rows[k], ((0,), (0,)))
 
-    for k in range(4):
-        m_ref[k * B : (k + 1) * B, k * B :] = d_ref[:, OFFSETS[k] : OFFSETS[k] + PANEL - k * B]
     inverses, uppers = [], []
+    summed_z = []
+    between = {1: lambda: (summed_z.append(pass_on_x()), pass_on_z(3)), 2: lambda: pass_on_z(0)}
     for k in range(4):
         if k == 1:
+            pass_on_z(2)
             pass_on_z(1)
-            pass_on_z(3)
-        if k == 2:
-            pass_on_z(0)
-            from_x = pass_on_x()
         if k == 3:
-            arrived(from_z)
-            upper_rows = rows(0, first_z[1] + first_z[2] + first_z[3])
+            summed_z[0].wait_recv()
+            upper_rows = rows(0, last_x[...])
             x_rows = [solved(0, upper_rows[0])]
             x_rows.append(solved(1, upper_rows[1] - under(0, 0, 1)))
             carried = under(0, 1, 3) + under(1, 0, 2)
         at = k * B
-        tiles = [m_ref[at + 8 * i : at + 8 * i + 8, at : at + B] for i in range(16)]
-        w = jnp.concatenate(inv_chol(tiles), axis=0)
+        if k == 0:
+            rest = []
+            tiles = [d_ref[8 * i : 8 * i + 8, :B] for i in range(16)]
+            tiles = inv_chol(tiles, lambda: rest.append(to_sibling(1)))
+            rest[0].wait_recv()
+            for r in range(4):
+                m_ref[r * B : (r + 1) * B, r * B :] = d_ref[:, OFFSETS[r] : OFFSETS[r] + PANEL - r * B]
+        else:
+            tiles = inv_chol([m_ref[at + 8 * i : at + 8 * i + 8, at : at + B] for i in range(16)], between.get(k))
+        w = jnp.concatenate(tiles, axis=0)
         inverses.append(w)
         if k == 3:
             break
@@ -324,8 +335,8 @@
         for r in range(k + 1, 4):
             left = u[:, (r - k - 1) * B : (r - k) * B]
             m_ref[r * B : (r + 1) * B, r * B :] -= dot(left, u[:, (r - k - 1) * B :], ((0,), (0,)))
-    from_x.wait_recv()
-    lower_rows = rows(1, last_x[...])
+    arrived(from_z)
+    lower_rows = rows(1, first_z[1] + first_z[2] + first_z[3])
     x_rows.append(solved(2, lower_rows[0] - carried[:B, :]))
     solved(3, lower_rows[1] - carried[B:, :] - under(2, 0, 1))
     for copy in sends:
@@ -366,7 +377,7 @@
             buf(HALF, SHARE),
             dma((4,)),
             *pair((2, 3)), *pair((2,)), *pair((2, 3)), *pair(), *pair((7,)), *pair((3,)), *pair(),
-            *pair((7,)), *pair(), *pair((2, RING, 2)), *pair((RING,)), *pair((RING,)), *pair((RING,)), *pair(),
+            *pair((2, 7)), *pair((2,)), *pair((2, RING)), *pair((RING,)), *pair((RING,)), *pair((RING,)), *pair(),
         ],
         compiler_params=pltpu.CompilerParams(collective_id=0, has_side_effects=True, vmem_limit_bytes=56 << 20),
     )(group_rows, panel_index, constraint_rows, shift.reshape(1, -1))

time: 59.8 us -> 58.6 us (0.980)
  Pallas kernels: 57.3 us -> 56 us
    pallas_call x1, Pallas kernels: 57.3 us -> 56 us  [panel_rows(): pl.pallas_call(panel_kernel, out_shape=jax.ShapeDtypeStruct((SHARE, PANEL...]
where the time goes in v5:
time: 58.6 us; the launch traced here: 58.4 us
  Pallas kernels  56 us (96%)
  local copies, waits for them, and re-layouts  1.67 us (3%)
  between operations  0.66 us (1%)
    pallas_call x1, Pallas kernels, panel_rows(): pl.pallas_call(panel_kernel, out_shape=jax.ShapeDtypeStruct((SHARE, PANEL...  56 us
    unnamed x1, local copies, waits for them, and re-layouts  1.67 us

profile of v5, /device:TPU:1, one launch (start us, length us, event | category | flops | bytes accessed | tf_op | source)
XLA Modules:
  0.0 58.4 jit_solution(6488685496513511638)
XLA Ops:
  0.7 56.0 %shard_map.46 = f32[128,512]{1,0:T(8,128)} custom-call(s32[16]{0:T(128)} %groups_hbm.1, s32[1]{0:T(128)S(6)} %copy.6.panel_hbm, f32[256,2048]{1,0:T(8,128)} %b_hbm.1, f32[1,2048]{1,0:T(1,128)} %bitcast.1), custom_call_target="tpu_custom_call" | custom-call | tf_op jit(solution)/shard_map/pallas_call | solution.py:351
  56.7 1.7 %copy.7 = f32[128,512]{1,0:T(8,128)} copy(f32[128,512]{1,0:T(8,128)} %shard_map.46) | data formatting | bytes 524288

commit v6 on v5

--- a/solution.py
+++ b/solution.py
@@ -351,7 +351,7 @@
     return pl.pallas_call(
         panel_kernel,
         out_shape=jax.ShapeDtypeStruct((SHARE, PANEL), f32),
-        in_specs=[pl.BlockSpec(memory_space=pl.ANY)] * 4,
+        in_specs=[pl.BlockSpec(memory_space=pltpu.HBM)] * 4,
         out_specs=pl.BlockSpec(memory_space=pltpu.VMEM),
         scratch_shapes=[
             pltpu.SMEM((16,), jnp.int32),
@@ -379,7 +379,7 @@
             *pair((2, 3)), *pair((2,)), *pair((2, 3)), *pair(), *pair((7,)), *pair((3,)), *pair(),
             *pair((2, 7)), *pair((2,)), *pair((2, RING)), *pair((RING,)), *pair((RING,)), *pair((RING,)), *pair(),
         ],
-        compiler_params=pltpu.CompilerParams(collective_id=0, has_side_effects=True, vmem_limit_bytes=56 << 20),
+        compiler_params=pltpu.CompilerParams(collective_id=0, has_side_effects=True, vmem_limit_bytes=53 << 20),
     )(group_rows, panel_index, constraint_rows, shift.reshape(1, -1))
 
 

time: 58.6 us -> 58.2 us (level)
  Pallas kernels: 56 us -> 55.3 us
    pallas_call x1, Pallas kernels: 56 us -> 55.3 us  [panel_rows(): pl.pallas_call(panel_kernel, out_shape=jax.ShapeDtypeStruct((SHARE, PANEL...]
    unnamed x1 -> x5, local copies, waits for them, and re-layouts: 1.67 us -> 2.05 us
where the time goes in v6:
time: 58.2 us; the launch traced here: 58 us
  Pallas kernels  55.3 us (95%)
  local copies, waits for them, and re-layouts  2.05 us (4%)
  between operations  0.67 us (1%)
    pallas_call x1, Pallas kernels, panel_rows(): pl.pallas_call(panel_kernel, out_shape=jax.ShapeDtypeStruct((SHARE, PANEL...  55.3 us
    unnamed x5, local copies, waits for them, and re-layouts  2.05 us

profile of v6, /device:TPU:1, one launch (start us, length us, event | category | flops | bytes accessed | tf_op | source)
XLA Modules:
  0.0 58.0 jit_solution(13991659295829779945)
XLA Ops:
  0.7 0.0 copy-start
  0.7 0.7 %copy-done = f32[2048]{0:T(1024)S(1)} copy-done((f32[2048]{0:T(1024)S(1)}, f32[2048]{0:T(1024)}, u32[]{:S(2)}) %copy-start) | copy-done | bytes 8216
  1.4 0.0 copy-start.1
  1.4 0.7 %copy-done.1 = s32[16]{0:T(128)S(1)} copy-done((s32[16]{0:T(128)S(1)}, s32[16]{0:T(128)}, u32[]{:S(2)}) %copy-start.1) | copy-done | bytes 88
  2.0 55.3 %shard_map.46 = f32[128,512]{1,0:T(8,128)S(1)} custom-call(s32[16]{0:T(128)S(1)} %copy-done.1, s32[1]{0:T(128)S(6)} %copy.6.panel_hbm, f32[256,2048]{1,0:T(8,128)} %b_hbm.1, f32[1,2048]{1,0:T(1,128)S(1)} %bitcast.1), custom_call_target="tpu_custom_call" | custom-call | tf_op jit(solution)/shard_map/pallas_call | solution.py:351
  57.3 0.7 %copy.7 = f32[128,512]{1,0:T(8,128)} copy(f32[128,512]{1,0:T(8,128)S(1)} %shard_map.46) | data formatting | bytes 524288
Async XLA Ops:
  0.7 0.7 %copy-start = (f32[2048]{0:T(1024)S(1)}, f32[2048]{0:T(1024)}, u32[]{:S(2)}) copy-start(f32[2048]{0:T(1024)} %param.5) | copy-start | bytes 24580
  1.4 0.7 %copy-start.1 = (s32[16]{0:T(128)S(1)}, s32[16]{0:T(128)}, u32[]{:S(2)}) copy-start(s32[16]{0:T(128)} %groups_hbm.1) | copy-start | bytes 196
